TPU v7x, 512 devices: a whole 4x4x16 slice. The times are simulated.
512 devices in a mesh: leaf: 16 (over z), panel: 32 (over y, x, core).
Axes of the slice: x: 4, y: 4, z: 16, core: 2. Of those that a mesh axis runs over, the one named last changes fastest.
Arguments:
- probe_low: bfloat16 [16, 4096, 256], P('leaf', 'panel'), may hold values from -6 to 6
- probe_mid: bfloat16 [16, 2048, 256], P('leaf', 'panel'), may hold values from -6 to 6
- probe_top: bfloat16 [16, 1024, 256], P('leaf', 'panel'), may hold values from -6 to 6
- inv_low: bfloat16 [16, 4096, 4096], P('leaf', 'panel'), may hold values from -0.09375 to 0.09375
- inv_mid: bfloat16 [16, 2048, 4096], P('leaf', 'panel'), may hold values from -0.09375 to 0.09375
- inv_top: bfloat16 [16, 1024, 4096], P('leaf', 'panel'), may hold values from -0.09375 to 0.09375
- gram_low: bfloat16 [16, 4096, 4096], P('leaf', 'panel'), may hold values from -0.09375 to 0.09375
- gram_mid: bfloat16 [16, 2048, 4096], P('leaf', 'panel'), may hold values from -0.09375 to 0.09375
- gram_top: bfloat16 [16, 1024, 4096], P('leaf', 'panel'), may hold values from -0.09375 to 0.09375
- panel_low: bfloat16 [16, 1024, 4096], P('leaf', 'panel'), may hold values from -0.09375 to 0.09375
- panel_mid: bfloat16 [16, 512, 4096], P('leaf', 'panel'), may hold values from -0.09375 to 0.09375
- back_low: bfloat16 [16, 4096, 1024], P('leaf', 'panel'), may hold values from -0.1875 to 0.1875
- back_mid: bfloat16 [16, 2048, 1024], P('leaf', 'panel'), may hold values from -0.1875 to 0.1875
- sep_low: int32 [16, 1024], replicated, may hold values from 0 to 4095, as said below
- sep_mid: int32 [8, 1024], replicated, may hold values from 0 to 4095, as said below
Outputs:
- half_low: bfloat16 [16, 4096, 256], P('leaf', 'panel')
- half_mid: bfloat16 [16, 2048, 256], P('leaf', 'panel')
- half_top: bfloat16 [16, 1024, 256], P('leaf', 'panel')
- solved_low: bfloat16 [16, 4096, 256], P('leaf', 'panel')
- solved_mid: bfloat16 [16, 2048, 256], P('leaf', 'panel')
- solved_top: bfloat16 [16, 1024, 256], P('leaf', 'panel')
Inputs may be any that keep to these rules, and one draw needn't show every extreme that they name: Each row of sep_low lists 1024 distinct rows of a parent supernode; 0 and 4095 occur in every row. Each row of sep_mid lists 1024 distinct rows of a parent supernode; 0 and 4095 occur in every row.
All inputs are finite; a program needn't handle non-finite values.
Results may differ from a plain program's by a relative error of at most 0.0085.
Values may be sent and summed in bfloat16 or wider, within the bound.
A program may use at most 64 MiB of HBM per device.

v0:
```python
import jax
import jax.numpy as jnp
from jax import lax
from jax.sharding import PartitionSpec as P


def from_partner(value, axis, bit):
    mask = 2**bit
    pairs = [(source, source ^ mask) for source in range(lax.axis_size(axis))]
    return lax.ppermute(value, axis, pairs)


def pair_up(block, bit):
    partner = from_partner(block, "leaf", bit)
    upper = lax.axis_index("leaf") >> bit & 1 == 1
    return jnp.where(
        upper, jnp.concatenate([partner, block], 0), jnp.concatenate([block, partner], 0)
    )


def sibling(block, bit):
    return from_partner(block, "leaf", bit)


def collect(piece, depth):
    whole = lax.all_gather(piece, "panel", axis=1, tiled=True)
    for bit in range(depth):
        whole = pair_up(whole, bit)
    return whole.reshape(-1, whole.shape[-1])


def product(matrix, rhs):
    return jnp.dot(matrix[0], rhs, preferred_element_type=jnp.float32)


def own_rows(full, depth, count):
    block = lax.axis_index("leaf") & (1 << depth) - 1
    start = (block * lax.axis_size("panel") + lax.axis_index("panel")) * count
    return lax.dynamic_slice_in_dim(full, start, count, 0)


def child_total(updates, other, rows_table, depth, height):
    child = lax.axis_index("leaf") >> depth
    own_map = lax.dynamic_index_in_dim(rows_table, child, 0, keepdims=False)
    other_map = lax.dynamic_index_in_dim(rows_table, child ^ 1, 0, keepdims=False)
    total = jnp.zeros((height, updates.shape[1]), jnp.float32)
    total = total.at[own_map].add(updates.astype(jnp.float32))
    return total.at[other_map].add(other.astype(jnp.float32))


def parent_side(updates, other, rows_table, depth, probe_local):
    count = probe_local.shape[1]
    total = child_total(
        updates, other, rows_table, depth, count * lax.axis_size("panel") * (2 << depth)
    )
    local = probe_local[0].astype(jnp.float32) - own_rows(total, depth + 1, count)
    return local.astype(jnp.bfloat16)[None]


def sweeps(
    probe_low,
    probe_mid,
    probe_top,
    inv_low,
    inv_mid,
    inv_top,
    gram_low,
    gram_mid,
    gram_top,
    panel_low,
    panel_mid,
    back_low,
    back_mid,
    sep_low,
    sep_mid,
):
    leaf_index = lax.axis_index("leaf")
    right_low = collect(probe_low, 0)
    update_low = product(panel_low, right_low).astype(jnp.bfloat16)
    update_low = collect(update_low[None], 0)
    right_mid = collect(parent_side(update_low, sibling(update_low, 0), sep_low, 0, probe_mid), 1)
    update_mid = product(panel_mid, right_mid).astype(jnp.bfloat16)
    update_mid = collect(update_mid[None], 1)
    right_top = collect(parent_side(update_mid, sibling(update_mid, 1), sep_mid, 1, probe_top), 2)
    half_low = product(inv_low, right_low).astype(jnp.bfloat16)
    half_mid = product(inv_mid, right_mid).astype(jnp.bfloat16)
    half_top = product(inv_top, right_top).astype(jnp.bfloat16)
    solved_top = product(gram_top, right_top).astype(jnp.bfloat16)
    parent_top = collect(solved_top[None], 2)
    map_mid = lax.dynamic_index_in_dim(sep_mid, leaf_index >> 1, 0, keepdims=False)
    taken_mid = jnp.take(parent_top, map_mid, axis=0)
    solved_mid = (product(gram_mid, right_mid) - product(back_mid, taken_mid)).astype(jnp.bfloat16)
    parent_mid = collect(solved_mid[None], 1)
    map_low = lax.dynamic_index_in_dim(sep_low, leaf_index, 0, keepdims=False)
    taken_low = jnp.take(parent_mid, map_low, axis=0)
    solved_low = (product(gram_low, right_low) - product(back_low, taken_low)).astype(jnp.bfloat16)
    return (
        half_low[None],
        half_mid[None],
        half_top[None],
        solved_low[None],
        solved_mid[None],
        solved_top[None],
    )


def body(
    probe_low,
    probe_mid,
    probe_top,
    inv_low,
    inv_mid,
    inv_top,
    gram_low,
    gram_mid,
    gram_top,
    panel_low,
    panel_mid,
    back_low,
    back_mid,
    sep_low,
    sep_mid,
):
    blocks_rest = (
        inv_low,
        inv_mid,
        inv_top,
        gram_low,
        gram_mid,
        gram_top,
        panel_low,
        panel_mid,
        back_low,
        back_mid,
        sep_low,
        sep_mid,
    )
    return sweeps(probe_low, probe_mid, probe_top, *blocks_rest)


def solution(mesh):
    return jax.shard_map(
        body,
        mesh=mesh,
        in_specs=(
            P("leaf", "panel", None),
            P("leaf", "panel", None),
            P("leaf", "panel", None),
            P("leaf", "panel", None),
            P("leaf", "panel", None),
            P("leaf", "panel", None),
            P("leaf", "panel", None),
            P("leaf", "panel", None),
            P("leaf", "panel", None),
            P("leaf", "panel", None),
            P("leaf", "panel", None),
            P("leaf", "panel", None),
            P("leaf", "panel", None),
            P(),
            P(),
        ),
        out_specs=(
            P("leaf", "panel", None),
            P("leaf", "panel", None),
            P("leaf", "panel", None),
            P("leaf", "panel", None),
            P("leaf", "panel", None),
            P("leaf", "panel", None),
        ),
        check_vma=False,
    )
```

profile of v0, /device:TPU:1, one launch (start us, length us, event | category | flops | bytes accessed | tf_op | source)
XLA Modules:
  0.0 584.4 jit_solution(5055272088833783193)
XLA Ops:
  8.0 68.1 %all-gather.10.cloned.1.call-done = bf16[1,4096,256]{2,1,0:T(8,128)(2,1)} async-done(((bf16[1,128,256]{2,1,0:T(8,128)(2,1)}), bf16[1,4096,256]{2,1,0:T(8,128)(2,1)}) %all-gather.10.cloned.1.call-update) | async-done | bytes 2097168 | tf_op jit(solution)/shard_map/all_gather | solution.py:26
  76.1 2.1 fusion.21
  78.2 24.0 %all-gather = bf16[1024,256]{1,0:T(8,128)(2,1)S(1)} all-gather(bf16[32,256]{1,0:T(8,128)(2,1)S(1)} %fusion.21), channel_id=2, replica_groups=mesh['leaf'=16,'panel'=32] {'panel'}, dimensions={0}, use_global_device_ids=true | all-gather | bytes 540672 | tf_op jit(solution)/shard_map/all_gather | solution.py:26
  102.2 3.2 collective-permute-start
  105.4 0.9 compare_select_fusion.2
  106.3 8.3 %scatter_custom_fusion = f32[4096,256]{1,0:T(8,128)} fusion(s32[1024]{0:T(1024)S(1)} %bitcast.132, f32[]{:T(128)} %constant.45.clone.1, bf16[1024,256]{1,0:T(8,128)(2,1)S(1)} %all-gather), kind=kCustom, calls=%fused_computation.18 | custom fusion | flops 524288 | bytes 4718596 | tf_op jit(solution)/shard_map/scatter-add | solution.py:47
  114.6 2.9 collective-permute-done
  117.5 10.2 %scatter_custom_fusion.1 = f32[4096,256]{1,0:T(8,128)} fusion(f32[4096,256]{1,0:T(8,128)} %scatter_custom_fusion, s32[1024]{0:T(1024)S(1)} %bitcast.131, bf16[1024,256]{1,0:T(8,128)(2,1)S(1)} %collective-permute-done), kind=kCustom, calls=%fused_computation.43 | custom fusion | flops 524288 | bytes 4718592 | tf_op jit(solution)/shard_map/scatter-add | solution.py:48
  127.7 1.5 fusion.49
  129.2 57.7 %all-gather.12.cloned.1.call-done = bf16[2048,256]{1,0:T(8,128)(2,1)} async-done(((bf16[64,256]{1,0:T(8,128)(2,1)}), bf16[2048,256]{1,0:T(8,128)(2,1)}) %all-gather.12.cloned.1.call-update) | async-done | bytes 1048592 | tf_op jit(solution)/shard_map/all_gather | solution.py:26
  186.9 3.2 collective-permute-start.1
  190.1 23.5 %collective-permute-done.1 = bf16[1,2048,256]{2,1,0:T(8,128)(2,1)} collective-permute-done((bf16[1,2048,256]{2,1,0:T(8,128)(2,1)}, bf16[1,2048,256]{2,1,0:T(8,128)(2,1)}, u32[]{:S(2)}, u32[]{:S(2)}) %collective-permute-start.1) | collective-permute-done | bytes 1048608 | tf_op jit(solution)/shard_map/ppermute | solution.py:10
  213.6 2.6 maximum_select_fusion
  216.6 24.9 %all-gather.2 = bf16[512,256]{1,0:T(8,128)(2,1)S(1)} all-gather(bf16[16,256]{1,0:T(8,128)(2,1)S(1)} %fusion.25), channel_id=4, replica_groups=mesh['leaf'=16,'panel'=32] {'panel'}, dimensions={0}, use_global_device_ids=true | all-gather | bytes 270336 | tf_op jit(solution)/shard_map/all_gather | solution.py:26
  241.6 3.2 collective-permute-start.2
  244.8 6.5 %collective-permute-done.2 = bf16[1,512,256]{2,1,0:T(8,128)(2,1)S(1)} collective-permute-done((bf16[1,512,256]{2,1,0:T(8,128)(2,1)S(1)}, bf16[1,512,256]{2,1,0:T(8,128)(2,1)S(1)}, u32[]{:S(2)}, u32[]{:S(2)}) %collective-permute-start.2) | collective-permute-done | bytes 262176 | tf_op jit(solution)/shard_map/ppermute | solution.py:10
  251.2 0.9 maximum_select_fusion.6
  252.1 4.3 collective-permute-start.3
  256.4 0.9 compare_select_fusion.1
  257.3 8.1 %scatter_custom_fusion.2 = f32[4096,256]{1,0:T(8,128)} fusion(s32[1024]{0:T(1024)S(1)} %bitcast.134, f32[]{:T(128)} %constant.45.clone.1, bf16[1024,256]{1,0:T(8,128)(2,1)} %bitcast.20), kind=kCustom, calls=%fused_computation.16 | custom fusion | flops 524288 | bytes 4718596 | tf_op jit(solution)/shard_map/scatter-add | solution.py:47
  265.4 13.8 %collective-permute-done.3 = bf16[1024,256]{1,0:T(8,128)(2,1)} collective-permute-done((bf16[1024,256]{1,0:T(8,128)(2,1)}, bf16[1024,256]{1,0:T(8,128)(2,1)}, u32[]{:S(2)}, u32[]{:S(2)}) %collective-permute-start.3) | collective-permute-done | bytes 524320 | tf_op jit(solution)/shard_map/ppermute | solution.py:10
  279.2 10.6 %scatter_custom_fusion.3 = f32[4096,256]{1,0:T(8,128)} fusion(f32[4096,256]{1,0:T(8,128)} %scatter_custom_fusion.2, s32[1024]{0:T(1024)S(1)} %bitcast.133, bf16[1024,256]{1,0:T(8,128)(2,1)} %collective-permute-done.3), kind=kCustom, calls=%fused_computation.40 | custom fusion | flops 524288 | bytes 4718592 | tf_op jit(solution)/shard_map/scatter-add | solution.py:48
  289.8 0.8 fusion.50
  290.6 24.0 %all-gather.3 = bf16[1024,256]{1,0:T(8,128)(2,1)S(1)} all-gather(bf16[32,256]{1,0:T(8,128)(2,1)S(1)} %fusion.50), channel_id=5, replica_groups=mesh['leaf'=16,'panel'=32] {'panel'}, dimensions={0}, use_global_device_ids=true | all-gather | bytes 540672 | tf_op jit(solution)/shard_map/all_gather | solution.py:26
  314.5 2.2 collective-permute-start.4
  316.8 13.0 %collective-permute-done.4 = bf16[1,1024,256]{2,1,0:T(8,128)(2,1)S(1)} collective-permute-done((bf16[1,1024,256]{2,1,0:T(8,128)(2,1)S(1)}, bf16[1,1024,256]{2,1,0:T(8,128)(2,1)S(1)}, u32[]{:S(2)}, u32[]{:S(2)}) %collective-permute-start.4) | collective-permute-done | bytes 524320 | tf_op jit(solution)/shard_map/ppermute | solution.py:10
  329.8 1.2 maximum_select_fusion.4
  330.9 4.1 collective-permute-start.5
  335.1 45.6 %collective-permute-done.5 = bf16[2,1024,256]{2,1,0:T(8,128)(2,1)} collective-permute-done((bf16[2,1024,256]{2,1,0:T(8,128)(2,1)}, bf16[2,1024,256]{2,1,0:T(8,128)(2,1)}, u32[]{:S(2)}, u32[]{:S(2)}) %collective-permute-start.5) | collective-permute-done | bytes 1048608 | tf_op jit(solution)/shard_map/ppermute | solution.py:10
  380.7 2.6 maximum_select_fusion.1
  383.8 25.3 %all-gather.4 = bf16[1024,256]{1,0:T(8,128)(2,1)S(1)} all-gather(bf16[32,256]{1,0:T(8,128)(2,1)S(1)} %bitcast.125), channel_id=6, replica_groups=mesh['leaf'=16,'panel'=32] {'panel'}, dimensions={0}, use_global_device_ids=true | all-gather | bytes 540672 | tf_op jit(solution)/shard_map/all_gather | solution.py:26
  409.1 2.2 collective-permute-start.6
  411.3 13.1 %collective-permute-done.6 = bf16[1,1024,256]{2,1,0:T(8,128)(2,1)S(1)} collective-permute-done((bf16[1,1024,256]{2,1,0:T(8,128)(2,1)S(1)}, bf16[1,1024,256]{2,1,0:T(8,128)(2,1)S(1)}, u32[]{:S(2)}, u32[]{:S(2)}) %collective-permute-start.6) | collective-permute-done | bytes 524320 | tf_op jit(solution)/shard_map/ppermute | solution.py:10
  424.5 4.1 collective-permute-start.7
  428.6 45.4 %collective-permute-done.7 = bf16[2,1024,256]{2,1,0:T(8,128)(2,1)S(1)} collective-permute-done((bf16[2,1024,256]{2,1,0:T(8,128)(2,1)S(1)}, bf16[2,1024,256]{2,1,0:T(8,128)(2,1)S(1)}, u32[]{:S(2)}, u32[]{:S(2)}) %collective-permute-start.7) | collective-permute-done | bytes 1048608 | tf_op jit(solution)/shard_map/ppermute | solution.py:10
  474.0 1.6 maximum_select_fusion.2
  475.7 6.5 %gather_fusion = bf16[1024,256]{1,0:T(8,128)(2,1)} fusion(bf16[4096,256]{1,0:T(8,128)(2,1)} %bitcast.111, s32[1024]{0:T(1024)S(1)} %fusion.51), kind=kCustom, calls=%fused_computation.clone | custom fusion | bytes 1052672 | tf_op jit(solution)/shard_map/jit(_take)/gather | solution.py:91
  482.1 1.4 fusion.37
  483.5 2.1 fusion.19
  485.7 0.8 constant_dynamic-slice_fusion
  486.5 57.2 %all-gather.14.cloned.1.call-done = bf16[2048,256]{1,0:T(8,128)(2,1)} async-done(((bf16[64,256]{1,0:T(8,128)(2,1)}), bf16[2048,256]{1,0:T(8,128)(2,1)}) %all-gather.14.cloned.1.call-update) | async-done | bytes 1048592 | tf_op jit(solution)/shard_map/all_gather | solution.py:26
  543.6 3.4 collective-permute-start.8
  547.1 2.7 fusion.16
  550.8 1.1 fusion.20
  552.4 1.1 fusion.24
  553.5 17.0 %collective-permute-done.8 = bf16[1,2048,256]{2,1,0:T(8,128)(2,1)S(1)} collective-permute-done((bf16[1,2048,256]{2,1,0:T(8,128)(2,1)}, bf16[1,2048,256]{2,1,0:T(8,128)(2,1)S(1)}, u32[]{:S(2)}, u32[]{:S(2)}) %collective-permute-start.8) | collective-permute-done | bytes 1048608 | tf_op jit(solution)/shard_map/ppermute | solution.py:10
  570.9 4.9 gather_fusion.1
  575.8 2.1 fusion.15
  (45 shorter events, 3.8 us)
Async XLA Ops:
  7.2 539.9 %copy-start = (bf16[1,128,4096]{2,1,0:T(8,128)(2,1)S(1)}, bf16[1,128,4096]{2,1,0:T(8,128)(2,1)}, u32[]{:S(2)}) copy-start(bf16[1,128,4096]{2,1,0:T(8,128)(2,1)} %param.20) | copy-start | bytes 3145732
  7.2 68.9 %all-gather.10.cloned.1.call-start = ((), (), s32[]{:S(2)}) async-start(), calls=%async_computation | async-start | bytes 2162688 | tf_op jit(solution)/shard_map/all_gather | solution.py:26
  7.9 179.0 %all-gather.12.cloned.1.call-start = ((), (), s32[]{:S(2)}) async-start(), calls=%async_computation.1 | async-start | bytes 1081344 | tf_op jit(solution)/shard_map/all_gather | solution.py:26
  102.2 15.3 %collective-permute-start = (bf16[1024,256]{1,0:T(8,128)(2,1)S(1)}, bf16[1024,256]{1,0:T(8,128)(2,1)S(1)}, u32[]{:S(2)}, u32[]{:S(2)}) collective-permute-start(bf16[1024,256]{1,0:T(8,128)(2,1)S(1)} %all-gather), channel_id=1, source_target_pairs={{0,32},{32,0},{64,96},{96,64},{128,160},{160,128},{192,224},{224,1... | collective-permute-start | bytes 1572872 | tf_op jit(solution)/shard_map/ppermute | solution.py:10
  117.5 10.2 %copy-start.11 = (bf16[1,64,256]{2,1,0:T(8,128)(2,1)S(1)}, bf16[1,64,256]{2,1,0:T(8,128)(2,1)}, u32[]{:S(2)}) copy-start(bf16[1,64,256]{2,1,0:T(8,128)(2,1)} %param.18) | copy-start | bytes 98308
  129.2 414.4 %all-gather.14.cloned.1.call-start = ((), (), s32[]{:S(2)}) async-start(), calls=%async_computation.2 | async-start | bytes 1081344 | tf_op jit(solution)/shard_map/all_gather | solution.py:26
  186.9 26.7 %collective-permute-start.1 = (bf16[1,2048,256]{2,1,0:T(8,128)(2,1)}, bf16[1,2048,256]{2,1,0:T(8,128)(2,1)}, u32[]{:S(2)}, u32[]{:S(2)}) collective-permute-start(bf16[1,2048,256]{2,1,0:T(8,128)(2,1)} %bitcast.119), channel_id=1, source_target_pairs={{0,32},{32,0},{64,96},{96,64},{128,160},{160,128},{192,224},{224,1... | collective-permute-start | bytes 3145736 | tf_op jit(solution)/shard_map/ppermute | solution.py:10
  190.1 26.2 %copy-start.9 = (bf16[1,16,4096]{2,1,0:T(8,128)(2,1)S(1)}, bf16[1,16,4096]{2,1,0:T(8,128)(2,1)}, u32[]{:S(2)}) copy-start(bf16[1,16,4096]{2,1,0:T(8,128)(2,1)} %param.27) | copy-start | bytes 393220
  241.6 9.6 %collective-permute-start.2 = (bf16[1,512,256]{2,1,0:T(8,128)(2,1)S(1)}, bf16[1,512,256]{2,1,0:T(8,128)(2,1)S(1)}, u32[]{:S(2)}, u32[]{:S(2)}) collective-permute-start(bf16[1,512,256]{2,1,0:T(8,128)(2,1)S(1)} %bitcast.121), channel_id=1, source_target_pairs={{0,32},{32,0},{64,96},{96,64},{128,160},{160,128},{192,224},{224,1... | collective-permute-start | bytes 786440 | tf_op jit(solution)/shard_map/ppermute | solution.py:10
  252.1 27.1 %collective-permute-start.3 = (bf16[1024,256]{1,0:T(8,128)(2,1)}, bf16[1024,256]{1,0:T(8,128)(2,1)}, u32[]{:S(2)}, u32[]{:S(2)}) collective-permute-start(bf16[1024,256]{1,0:T(8,128)(2,1)} %bitcast.20), channel_id=1, source_target_pairs={{0,64},{32,96},{64,0},{96,32},{128,192},{160,224},{192,128},{224,1... | collective-permute-start | bytes 1572872 | tf_op jit(solution)/shard_map/ppermute | solution.py:10
  279.2 10.6 %copy-start.12 = (bf16[1,32,256]{2,1,0:T(8,128)(2,1)S(1)}, bf16[1,32,256]{2,1,0:T(8,128)(2,1)}, u32[]{:S(2)}) copy-start(bf16[1,32,256]{2,1,0:T(8,128)(2,1)} %param.19) | copy-start | bytes 49156
  314.5 15.3 %collective-permute-start.4 = (bf16[1,1024,256]{2,1,0:T(8,128)(2,1)S(1)}, bf16[1,1024,256]{2,1,0:T(8,128)(2,1)S(1)}, u32[]{:S(2)}, u32[]{:S(2)}) collective-permute-start(bf16[1,1024,256]{2,1,0:T(8,128)(2,1)S(1)} %bitcast.113), channel_id=1, source_target_pairs={{0,32},{32,0},{64,96},{96,64},{128,160},{160,128},{192,224},{224,1... | collective-permute-start | bytes 1572872 | tf_op jit(solution)/shard_map/ppermute | solution.py:10
  330.9 49.8 %collective-permute-start.5 = (bf16[2,1024,256]{2,1,0:T(8,128)(2,1)}, bf16[2,1024,256]{2,1,0:T(8,128)(2,1)}, u32[]{:S(2)}, u32[]{:S(2)}) collective-permute-start(bf16[2,1024,256]{2,1,0:T(8,128)(2,1)} %maximum_select_fusion.4), channel_id=1, source_target_pairs={{0,64},{32,96},{64,0},{96,32},{128,192},{160,224},{192,128},{224,1... | collective-permute-start | bytes 3145736 | tf_op jit(solution)/shard_map/ppermute | solution.py:10
  335.1 48.3 %copy-start.7 = (bf16[1,32,4096]{2,1,0:T(8,128)(2,1)S(1)}, bf16[1,32,4096]{2,1,0:T(8,128)(2,1)}, u32[]{:S(2)}) copy-start(bf16[1,32,4096]{2,1,0:T(8,128)(2,1)} %param.25) | copy-start | bytes 786436
  383.3 41.2 %copy-start.2 = (bf16[4,1024,256]{2,1,0:T(8,128)(2,1)}, bf16[4,1024,256]{2,1,0:T(8,128)(2,1)S(1)}, u32[]{:S(2)}) copy-start(bf16[4,1024,256]{2,1,0:T(8,128)(2,1)S(1)} %maximum_select_fusion.1) | copy-start | bytes 6291460
  383.8 91.9 %copy-start.10 = (bf16[256,32]{0,1:T(8,128)(2,1)}, bf16[256,32]{0,1:T(8,128)(2,1)S(1)}, u32[]{:S(2)}) copy-start(bf16[256,32]{0,1:T(8,128)(2,1)S(1)} %convolution_convert_fusion.1) | copy-start | bytes 49156
  409.1 15.3 %collective-permute-start.6 = (bf16[1,1024,256]{2,1,0:T(8,128)(2,1)S(1)}, bf16[1,1024,256]{2,1,0:T(8,128)(2,1)S(1)}, u32[]{:S(2)}, u32[]{:S(2)}) collective-permute-start(bf16[1,1024,256]{2,1,0:T(8,128)(2,1)S(1)} %bitcast.115), channel_id=1, source_target_pairs={{0,32},{32,0},{64,96},{96,64},{128,160},{160,128},{192,224},{224,1... | collective-permute-start | bytes 1572872 | tf_op jit(solution)/shard_map/ppermute | solution.py:10
  424.5 49.5 %collective-permute-start.7 = (bf16[2,1024,256]{2,1,0:T(8,128)(2,1)S(1)}, bf16[2,1024,256]{2,1,0:T(8,128)(2,1)S(1)}, u32[]{:S(2)}, u32[]{:S(2)}) collective-permute-start(bf16[2,1024,256]{2,1,0:T(8,128)(2,1)S(1)} %maximum_select_fusion.5), channel_id=1, source_target_pairs={{0,64},{32,96},{64,0},{96,32},{128,192},{160,224},{192,128},{224,1... | collective-permute-start | bytes 3145736 | tf_op jit(solution)/shard_map/ppermute | solution.py:10
  475.7 6.5 %copy-start.14 = (bf16[1,64,1024]{2,1,0:T(8,128)(2,1)S(1)}, bf16[1,64,1024]{2,1,0:T(8,128)(2,1)}, u32[]{:S(2)}) copy-start(bf16[1,64,1024]{2,1,0:T(8,128)(2,1)} %param.29) | copy-start | bytes 393220
  543.6 6.1 %copy-start.1 = (bf16[1,4096,256]{2,1,0:T(8,128)(2,1)S(1)}, bf16[1,4096,256]{2,1,0:T(8,128)(2,1)}, u32[]{:S(2)}) copy-start(bf16[1,4096,256]{2,1,0:T(8,128)(2,1)} %all-gather.10.cloned.1.call-done) | copy-start | bytes 6291460
  543.6 6.1 %copy-start.4 = (bf16[1,128,4096]{2,1,0:T(8,128)(2,1)S(1)}, bf16[1,128,4096]{2,1,0:T(8,128)(2,1)}, u32[]{:S(2)}) copy-start(bf16[1,128,4096]{2,1,0:T(8,128)(2,1)} %param.23) | copy-start | bytes 3145732
  543.6 26.9 %collective-permute-start.8 = (bf16[1,2048,256]{2,1,0:T(8,128)(2,1)}, bf16[1,2048,256]{2,1,0:T(8,128)(2,1)S(1)}, u32[]{:S(2)}, u32[]{:S(2)}) collective-permute-start(bf16[1,2048,256]{2,1,0:T(8,128)(2,1)} %bitcast.117), channel_id=1, source_target_pairs={{0,32},{32,0},{64,96},{96,64},{128,160},{160,128},{192,224},{224,1... | collective-permute-start | bytes 3145736 | tf_op jit(solution)/shard_map/ppermute | solution.py:10
  549.8 1.0 copy-start.6
  549.8 2.1 copy-start.8
  550.8 1.6 copy-start.3
  550.8 19.7 %copy-start.5 = (bf16[2048,256]{1,0:T(8,128)(2,1)S(1)}, bf16[2048,256]{1,0:T(8,128)(2,1)}, u32[]{:S(2)}) copy-start(bf16[2048,256]{1,0:T(8,128)(2,1)} %all-gather.14.cloned.1.call-done) | copy-start | bytes 3145732
  570.9 5.0 copy-start.13
Sparse Core Ops, SparseCore 0:
  11.2 64.8 all-gather.9
  129.3 57.5 all-gather.11
  485.8 57.7 all-gather.13
where the time goes:
time: 585 us; the launch traced here: 584 us
  waiting for transfers between devices  364 us (62%)
  blocking collectives  98.2 us (17%)
  other arithmetic  50.5 us (9%)
  starting transfers between devices  30.1 us (5%)
  between operations  14 us (2%)
  matrix products  13.8 us (2%)
  local copies, waits for them, and re-layouts  13.4 us (2%)
    all_gather x3, waiting for transfers between devices, collect(): whole = lax.all_gather(piece, 'panel', axis=1, tiled=True)  183 us
    ppermute x9, waiting for transfers between devices, from_partner(): return lax.ppermute(value, axis, pairs)  181 us
    all_gather x4, blocking collectives, collect(): whole = lax.all_gather(piece, 'panel', axis=1, tiled=True)  98.2 us
    ppermute x9, starting transfers between devices, from_partner(): return lax.ppermute(value, axis, pairs)  29.9 us
    scatter-add x2, other arithmetic, child_total(): return total.at[other_map].add(other.astype(jnp.float32))  20.8 us
    scatter-add x2, other arithmetic, child_total(): total = total.at[own_map].add(updates.astype(jnp.float32))  16.4 us
    dot_general x10, matrix products, product(): return jnp.dot(matrix[0], rhs, preferred_element_type=jnp.float32)  13.8 us
  transfers between devices with their start and end apart: 12, of which 12 were waited for; matrix products, arithmetic and copies ran while one was open for 4% of the time, Pallas kernels for 0%

commit v1 on v0

--- a/solution.py
+++ b/solution.py
@@ -23,7 +23,9 @@
 
 
 def collect(piece, depth):
-    whole = lax.all_gather(piece, "panel", axis=1, tiled=True)
+    whole = jnp.concatenate(
+        lax.all_to_all(jnp.stack([piece] * lax.axis_size("panel")), "panel", 0, 0), axis=1
+    )
     for bit in range(depth):
         whole = pair_up(whole, bit)
     return whole.reshape(-1, whole.shape[-1])

time: 585 us -> 438 us (0.75)
  waiting for transfers between devices: 364 us -> 205 us
  blocking collectives: 98.2 us -> 122 us
  between operations: 14 us -> 0.96 us
    all_gather x3 -> x0, waiting for transfers between devices: 183 us -> none  [collect(): whole = lax.all_gather(piece, 'panel', axis=1, tiled=True)]
    all_to_all x0 -> x6, blocking collectives: none -> 122 us  [collect(): lax.all_to_all(jnp.stack([piece] * lax.axis_size('panel')), 'panel', 0, 0)]
    all_gather x4 -> x0, blocking collectives: 98.2 us -> none  [collect(): whole = lax.all_gather(piece, 'panel', axis=1, tiled=True)]
    all_to_all x0 -> x1, waiting for transfers between devices: none -> 16.6 us  [collect(): lax.all_to_all(jnp.stack([piece] * lax.axis_size('panel')), 'panel', 0, 0)]
    ppermute x9, waiting for transfers between devices: 181 us -> 189 us  [from_partner(): return lax.ppermute(value, axis, pairs)]
    ppermute x9, starting transfers between devices: 29.9 us -> 23.4 us  [from_partner(): return lax.ppermute(value, axis, pairs)]
  transfers between devices with their start and end apart: 12 -> 10, of which waited for: 12 -> 10; matrix products, arithmetic and copies ran while one was open for 4% -> 5% of each run, Pallas kernels for 0% -> 0%
where the time goes in v1:
time: 438 us; the launch traced here: 436 us
  waiting for transfers between devices  205 us (47%)
  blocking collectives  122 us (28%)
  other arithmetic  51.7 us (12%)
  starting transfers between devices  28.2 us (6%)
  local copies, waits for them, and re-layouts  17.9 us (4%)
  matrix products  10.7 us (2%)
    ppermute x9, waiting for transfers between devices, from_partner(): return lax.ppermute(value, axis, pairs)  189 us
    all_to_all x6, blocking collectives, collect(): lax.all_to_all(jnp.stack([piece] * lax.axis_size('panel')), 'panel', 0, 0)  122 us
    ppermute x9, starting transfers between devices, from_partner(): return lax.ppermute(value, axis, pairs)  23.4 us
    scatter-add x2, other arithmetic, child_total(): return total.at[other_map].add(other.astype(jnp.float32))  21.2 us
    all_to_all x1, waiting for transfers between devices, collect(): lax.all_to_all(jnp.stack([piece] * lax.axis_size('panel')), 'panel', 0, 0)  16.6 us
    scatter-add x2, other arithmetic, child_total(): total = total.at[own_map].add(updates.astype(jnp.float32))  16.3 us
    select_n x7, other arithmetic, pair_up(): jnp.where(upper, jnp.concatenate([partner, block], 0), jnp.concatenate([b...  10.8 us
    dot_general x10, matrix products, product(): return jnp.dot(matrix[0], rhs, preferred_element_type=jnp.float32)  10.7 us
  transfers between devices with their start and end apart: 10, of which 10 were waited for; matrix products, arithmetic and copies ran while one was open for 5% of the time, Pallas kernels for 0%

profile of v1, /device:TPU:1, one launch (start us, length us, event | category | flops | bytes accessed | tf_op | source)
XLA Modules:
  0.0 436.4 jit_solution(11515218564930025843)
XLA Ops:
  0.6 1.2 stack.14
  1.8 38.2 %all_to_all.35 = bf16[32,1,128,256]{3,2,1,0:T(8,128)(2,1)S(1)} all-to-all(bf16[32,1,128,256]{3,2,1,0:T(8,128)(2,1)S(1)} %stack.14), channel_id=1, replica_groups=mesh['leaf'=16,'panel'=32] {'panel'}, dimensions={0} | all-to-all | bytes 4194304 | tf_op jit(solution)/shard_map/all_to_all | solution.py:27
  40.6 15.4 %all_to_all.36 = bf16[32,1,32,256]{3,2,1,0:T(8,128)(2,1)} all-to-all(bf16[32,1,32,256]{3,2,1,0:T(8,128)(2,1)S(1)} %stack.15), channel_id=1, replica_groups=mesh['leaf'=16,'panel'=32] {'panel'}, dimensions={0} | all-to-all | bytes 1048576 | tf_op jit(solution)/shard_map/all_to_all | solution.py:27
  55.9 2.3 collective-permute-start
  59.1 8.2 %scatter_custom_fusion = f32[4096,256]{1,0:T(8,128)} fusion(s32[1024]{0:T(1024)S(1)} %bitcast.125, f32[]{:T(128)} %constant.45.clone.1, bf16[1024,256]{1,0:T(8,128)(2,1)} %bitcast.8), kind=kCustom, calls=%fused_computation.12 | custom fusion | flops 524288 | bytes 4718596 | tf_op jit(solution)/shard_map/scatter-add | solution.py:49
  67.2 4.0 collective-permute-done
  71.2 10.6 %scatter_custom_fusion.1 = f32[4096,256]{1,0:T(8,128)} fusion(f32[4096,256]{1,0:T(8,128)} %scatter_custom_fusion, s32[1024]{0:T(1024)S(1)} %bitcast.124, bf16[1024,256]{1,0:T(8,128)(2,1)} %collective-permute-done), kind=kCustom, calls=%fused_computation.38 | custom fusion | flops 524288 | bytes 4718592 | tf_op jit(solution)/shard_map/scatter-add | solution.py:50
  82.8 21.9 %all_to_all.37 = bf16[32,1,64,256]{3,2,1,0:T(8,128)(2,1)} all-to-all(bf16[32,1,64,256]{3,2,1,0:T(8,128)(2,1)S(1)} %stack.16), channel_id=1, replica_groups=mesh['leaf'=16,'panel'=32] {'panel'}, dimensions={0} | all-to-all | bytes 2097152 | tf_op jit(solution)/shard_map/all_to_all | solution.py:27
  104.7 2.3 collective-permute-start.1
  107.0 24.3 %collective-permute-done.1 = bf16[1,2048,256]{2,1,0:T(8,128)(2,1)} collective-permute-done((bf16[1,2048,256]{2,1,0:T(8,128)(2,1)}, bf16[1,2048,256]{2,1,0:T(8,128)(2,1)}, u32[]{:S(2)}, u32[]{:S(2)}) %collective-permute-start.1) | collective-permute-done | bytes 1048608 | tf_op jit(solution)/shard_map/ppermute | solution.py:10
  131.2 2.6 maximum_select_fusion
  133.8 1.3 copy-done.1
  135.6 13.2 %all_to_all.38 = bf16[32,1,16,256]{3,2,1,0:T(8,128)(2,1)S(1)} all-to-all(bf16[32,1,16,256]{3,2,1,0:T(8,128)(2,1)S(1)} %stack.17), channel_id=1, replica_groups=mesh['leaf'=16,'panel'=32] {'panel'}, dimensions={0} | all-to-all | bytes 524288 | tf_op jit(solution)/shard_map/all_to_all | solution.py:27
  148.8 2.3 collective-permute-start.2
  151.1 7.3 %collective-permute-done.2 = bf16[1,512,256]{2,1,0:T(8,128)(2,1)S(1)} collective-permute-done((bf16[1,512,256]{2,1,0:T(8,128)(2,1)S(1)}, bf16[1,512,256]{2,1,0:T(8,128)(2,1)S(1)}, u32[]{:S(2)}, u32[]{:S(2)}) %collective-permute-start.2) | collective-permute-done | bytes 262176 | tf_op jit(solution)/shard_map/ppermute | solution.py:10
  158.4 0.9 maximum_select_fusion.6
  159.2 3.8 collective-permute-start.3
  163.9 8.2 %scatter_custom_fusion.2 = f32[4096,256]{1,0:T(8,128)} fusion(s32[1024]{0:T(1024)S(1)} %bitcast.127, f32[]{:T(128)} %constant.45.clone.1, bf16[1024,256]{1,0:T(8,128)(2,1)} %bitcast.22), kind=kCustom, calls=%fused_computation.10 | custom fusion | flops 524288 | bytes 4718596 | tf_op jit(solution)/shard_map/scatter-add | solution.py:49
  172.1 14.6 %collective-permute-done.3 = bf16[1024,256]{1,0:T(8,128)(2,1)} collective-permute-done((bf16[1024,256]{1,0:T(8,128)(2,1)}, bf16[1024,256]{1,0:T(8,128)(2,1)}, u32[]{:S(2)}, u32[]{:S(2)}) %collective-permute-start.3) | collective-permute-done | bytes 524320 | tf_op jit(solution)/shard_map/ppermute | solution.py:10
  186.6 10.6 %scatter_custom_fusion.3 = f32[4096,256]{1,0:T(8,128)} fusion(f32[4096,256]{1,0:T(8,128)} %scatter_custom_fusion.2, s32[1024]{0:T(1024)S(1)} %bitcast.126, bf16[1024,256]{1,0:T(8,128)(2,1)} %collective-permute-done.3), kind=kCustom, calls=%fused_computation.35 | custom fusion | flops 524288 | bytes 4718592 | tf_op jit(solution)/shard_map/scatter-add | solution.py:50
  198.1 16.4 %all_to_all.39 = bf16[32,1,32,256]{3,2,1,0:T(8,128)(2,1)S(1)} all-to-all(bf16[32,1,32,256]{3,2,1,0:T(8,128)(2,1)S(1)} %stack.18), channel_id=1, replica_groups=mesh['leaf'=16,'panel'=32] {'panel'}, dimensions={0} | all-to-all | bytes 1048576 | tf_op jit(solution)/shard_map/all_to_all | solution.py:27
  214.5 1.9 collective-permute-start.4
  216.4 13.0 %collective-permute-done.4 = bf16[1,1024,256]{2,1,0:T(8,128)(2,1)S(1)} collective-permute-done((bf16[1,1024,256]{2,1,0:T(8,128)(2,1)S(1)}, bf16[1,1024,256]{2,1,0:T(8,128)(2,1)S(1)}, u32[]{:S(2)}, u32[]{:S(2)}) %collective-permute-start.4) | collective-permute-done | bytes 524320 | tf_op jit(solution)/shard_map/ppermute | solution.py:10
  229.4 1.1 maximum_select_fusion.4
  230.6 3.8 collective-permute-start.5
  234.4 46.3 %collective-permute-done.5 = bf16[2,1024,256]{2,1,0:T(8,128)(2,1)} collective-permute-done((bf16[2,1024,256]{2,1,0:T(8,128)(2,1)}, bf16[2,1024,256]{2,1,0:T(8,128)(2,1)}, u32[]{:S(2)}, u32[]{:S(2)}) %collective-permute-start.5) | collective-permute-done | bytes 1048608 | tf_op jit(solution)/shard_map/ppermute | solution.py:10
  280.7 2.6 maximum_select_fusion.1
  283.8 16.6 %all_to_all.40 = bf16[32,1,32,256]{3,2,1,0:T(8,128)(2,1)S(1)} all-to-all(bf16[32,1,32,256]{3,2,1,0:T(8,128)(2,1)S(1)} %stack.19), channel_id=1, replica_groups=mesh['leaf'=16,'panel'=32] {'panel'}, dimensions={0} | all-to-all | bytes 1048576 | tf_op jit(solution)/shard_map/all_to_all | solution.py:27
  300.4 1.9 collective-permute-start.6
  302.4 13.0 %collective-permute-done.6 = bf16[1,1024,256]{2,1,0:T(8,128)(2,1)S(1)} collective-permute-done((bf16[1,1024,256]{2,1,0:T(8,128)(2,1)S(1)}, bf16[1,1024,256]{2,1,0:T(8,128)(2,1)S(1)}, u32[]{:S(2)}, u32[]{:S(2)}) %collective-permute-start.6) | collective-permute-done | bytes 524320 | tf_op jit(solution)/shard_map/ppermute | solution.py:10
  315.6 3.1 collective-permute-start.7
  318.7 47.1 %collective-permute-done.7 = bf16[2,1024,256]{2,1,0:T(8,128)(2,1)S(1)} collective-permute-done((bf16[2,1024,256]{2,1,0:T(8,128)(2,1)S(1)}, bf16[2,1024,256]{2,1,0:T(8,128)(2,1)S(1)}, u32[]{:S(2)}, u32[]{:S(2)}) %collective-permute-start.7) | collective-permute-done | bytes 1048608 | tf_op jit(solution)/shard_map/ppermute | solution.py:10
  365.9 1.6 maximum_select_fusion.2
  367.5 6.5 %gather_fusion = bf16[1024,256]{1,0:T(8,128)(2,1)} fusion(bf16[4096,256]{1,0:T(8,128)(2,1)} %bitcast.107, s32[1024]{0:T(1024)S(1)} %fusion.38), kind=kCustom, calls=%fused_computation.clone | custom fusion | bytes 1052672 | tf_op jit(solution)/shard_map/jit(_take)/gather | solution.py:93
  374.0 1.4 fusion.24
  375.4 2.2 fusion.8
  377.6 1.1 stack.20
  378.8 4.8 %all-to-all-start.6 = ((bf16[32,1,64,256]{3,2,1,0:T(8,128)(2,1)}), bf16[32,1,64,256]{3,2,1,0:T(8,128)(2,1)}, u32[]{:S(2)}, u32[]{:S(2)}) async-start(bf16[32,1,64,256]{3,2,1,0:T(8,128)(2,1)} %stack.20), calls=%async_computation.6 | async-start | bytes 2097152 | tf_op jit(solution)/shard_map/all_to_all | solution.py:27
  384.4 16.6 %all-to-all-done.6 = bf16[32,1,64,256]{3,2,1,0:T(8,128)(2,1)} async-done(((bf16[32,1,64,256]{3,2,1,0:T(8,128)(2,1)}), bf16[32,1,64,256]{3,2,1,0:T(8,128)(2,1)}, u32[]{:S(2)}, u32[]{:S(2)}) %all-to-all-start.6) | async-done | bytes 1048608 | tf_op jit(solution)/shard_map/all_to_all | solution.py:27
  400.9 2.0 collective-permute-start.8
  403.0 1.1 fusion.7
  404.5 1.1 copy-done.2
  405.7 1.1 fusion.9
  407.4 1.1 fusion.10
  408.4 19.1 %collective-permute-done.8 = bf16[1,2048,256]{2,1,0:T(8,128)(2,1)S(1)} collective-permute-done((bf16[1,2048,256]{2,1,0:T(8,128)(2,1)}, bf16[1,2048,256]{2,1,0:T(8,128)(2,1)S(1)}, u32[]{:S(2)}, u32[]{:S(2)}) %collective-permute-start.8) | collective-permute-done | bytes 1048608 | tf_op jit(solution)/shard_map/ppermute | solution.py:10
  427.5 1.9 maximum_select_fusion.3
  429.3 4.9 %gather_fusion.1 = bf16[1024,256]{1,0:T(8,128)(2,1)} fusion(bf16[4096,256]{1,0:T(8,128)(2,1)S(1)} %bitcast.108, s32[1024]{0:T(1024)S(1)} %fusion.39), kind=kCustom, calls=%fused_computation.1.clone | custom fusion | bytes 1052672 | tf_op jit(solution)/shard_map/jit(_take)/gather | solution.py:97
  434.3 2.1 fusion.6
  (49 shorter events, 7.0 us)
Async XLA Ops:
  0.6 402.3 %copy-start = (bf16[1,128,4096]{2,1,0:T(8,128)(2,1)S(1)}, bf16[1,128,4096]{2,1,0:T(8,128)(2,1)}, u32[]{:S(2)}) copy-start(bf16[1,128,4096]{2,1,0:T(8,128)(2,1)} %param.20) | copy-start | bytes 3145732
  1.8 38.2 %copy-start.7 = (bf16[1,32,4096]{2,1,0:T(8,128)(2,1)S(1)}, bf16[1,32,4096]{2,1,0:T(8,128)(2,1)}, u32[]{:S(2)}) copy-start(bf16[1,32,4096]{2,1,0:T(8,128)(2,1)} %param.26) | copy-start | bytes 786436
  55.9 15.2 %collective-permute-start = (bf16[1024,256]{1,0:T(8,128)(2,1)}, bf16[1024,256]{1,0:T(8,128)(2,1)}, u32[]{:S(2)}, u32[]{:S(2)}) collective-permute-start(bf16[1024,256]{1,0:T(8,128)(2,1)} %bitcast.8), channel_id=1, source_target_pairs={{0,32},{32,0},{64,96},{96,64},{128,160},{160,128},{192,224},{224,1... | collective-permute-start | bytes 1572872 | tf_op jit(solution)/shard_map/ppermute | solution.py:10
  71.2 10.6 %copy-start.13 = (bf16[1,64,256]{2,1,0:T(8,128)(2,1)S(1)}, bf16[1,64,256]{2,1,0:T(8,128)(2,1)}, u32[]{:S(2)}) copy-start(bf16[1,64,256]{2,1,0:T(8,128)(2,1)} %param.18) | copy-start | bytes 98308
  104.7 26.5 %collective-permute-start.1 = (bf16[1,2048,256]{2,1,0:T(8,128)(2,1)}, bf16[1,2048,256]{2,1,0:T(8,128)(2,1)}, u32[]{:S(2)}, u32[]{:S(2)}) collective-permute-start(bf16[1,2048,256]{2,1,0:T(8,128)(2,1)} %bitcast.11), channel_id=1, source_target_pairs={{0,32},{32,0},{64,96},{96,64},{128,160},{160,128},{192,224},{224,1... | collective-permute-start | bytes 3145736 | tf_op jit(solution)/shard_map/ppermute | solution.py:10
  107.0 28.2 %copy-start.11 = (bf16[1,16,4096]{2,1,0:T(8,128)(2,1)S(1)}, bf16[1,16,4096]{2,1,0:T(8,128)(2,1)}, u32[]{:S(2)}) copy-start(bf16[1,16,4096]{2,1,0:T(8,128)(2,1)} %param.27) | copy-start | bytes 393220
  133.8 1.4 copy-start.1
  148.8 9.6 %collective-permute-start.2 = (bf16[1,512,256]{2,1,0:T(8,128)(2,1)S(1)}, bf16[1,512,256]{2,1,0:T(8,128)(2,1)S(1)}, u32[]{:S(2)}, u32[]{:S(2)}) collective-permute-start(bf16[1,512,256]{2,1,0:T(8,128)(2,1)S(1)} %bitcast.113), channel_id=1, source_target_pairs={{0,32},{32,0},{64,96},{96,64},{128,160},{160,128},{192,224},{224,1... | collective-permute-start | bytes 786440 | tf_op jit(solution)/shard_map/ppermute | solution.py:10
  159.2 27.4 %collective-permute-start.3 = (bf16[1024,256]{1,0:T(8,128)(2,1)}, bf16[1024,256]{1,0:T(8,128)(2,1)}, u32[]{:S(2)}, u32[]{:S(2)}) collective-permute-start(bf16[1024,256]{1,0:T(8,128)(2,1)} %bitcast.22), channel_id=1, source_target_pairs={{0,64},{32,96},{64,0},{96,32},{128,192},{160,224},{192,128},{224,1... | collective-permute-start | bytes 1572872 | tf_op jit(solution)/shard_map/ppermute | solution.py:10
  186.6 10.6 %copy-start.14 = (bf16[1,32,256]{2,1,0:T(8,128)(2,1)S(1)}, bf16[1,32,256]{2,1,0:T(8,128)(2,1)}, u32[]{:S(2)}) copy-start(bf16[1,32,256]{2,1,0:T(8,128)(2,1)} %param.19) | copy-start | bytes 49156
  214.5 14.9 %collective-permute-start.4 = (bf16[1,1024,256]{2,1,0:T(8,128)(2,1)S(1)}, bf16[1,1024,256]{2,1,0:T(8,128)(2,1)S(1)}, u32[]{:S(2)}, u32[]{:S(2)}) collective-permute-start(bf16[1,1024,256]{2,1,0:T(8,128)(2,1)S(1)} %bitcast.109), channel_id=1, source_target_pairs={{0,32},{32,0},{64,96},{96,64},{128,160},{160,128},{192,224},{224,1... | collective-permute-start | bytes 1572872 | tf_op jit(solution)/shard_map/ppermute | solution.py:10
  230.6 50.1 %collective-permute-start.5 = (bf16[2,1024,256]{2,1,0:T(8,128)(2,1)}, bf16[2,1024,256]{2,1,0:T(8,128)(2,1)}, u32[]{:S(2)}, u32[]{:S(2)}) collective-permute-start(bf16[2,1024,256]{2,1,0:T(8,128)(2,1)} %maximum_select_fusion.4), channel_id=1, source_target_pairs={{0,64},{32,96},{64,0},{96,32},{128,192},{160,224},{192,128},{224,1... | collective-permute-start | bytes 3145736 | tf_op jit(solution)/shard_map/ppermute | solution.py:10
  234.4 48.9 %copy-start.8 = (bf16[1,32,4096]{2,1,0:T(8,128)(2,1)S(1)}, bf16[1,32,4096]{2,1,0:T(8,128)(2,1)}, u32[]{:S(2)}) copy-start(bf16[1,32,4096]{2,1,0:T(8,128)(2,1)} %param.25) | copy-start | bytes 786436
  283.3 32.3 %copy-start.3 = (bf16[4,1024,256]{2,1,0:T(8,128)(2,1)}, bf16[4,1024,256]{2,1,0:T(8,128)(2,1)S(1)}, u32[]{:S(2)}) copy-start(bf16[4,1024,256]{2,1,0:T(8,128)(2,1)S(1)} %maximum_select_fusion.1) | copy-start | bytes 6291460
  283.7 83.8 %copy-start.12 = (bf16[256,32]{0,1:T(8,128)(2,1)}, bf16[256,32]{0,1:T(8,128)(2,1)S(1)}, u32[]{:S(2)}) copy-start(bf16[256,32]{0,1:T(8,128)(2,1)S(1)} %convolution_convert_fusion.2) | copy-start | bytes 49156
  300.4 14.9 %collective-permute-start.6 = (bf16[1,1024,256]{2,1,0:T(8,128)(2,1)S(1)}, bf16[1,1024,256]{2,1,0:T(8,128)(2,1)S(1)}, u32[]{:S(2)}, u32[]{:S(2)}) collective-permute-start(bf16[1,1024,256]{2,1,0:T(8,128)(2,1)S(1)} %bitcast.111), channel_id=1, source_target_pairs={{0,32},{32,0},{64,96},{96,64},{128,160},{160,128},{192,224},{224,1... | collective-permute-start | bytes 1572872 | tf_op jit(solution)/shard_map/ppermute | solution.py:10
  315.6 50.3 %collective-permute-start.7 = (bf16[2,1024,256]{2,1,0:T(8,128)(2,1)S(1)}, bf16[2,1024,256]{2,1,0:T(8,128)(2,1)S(1)}, u32[]{:S(2)}, u32[]{:S(2)}) collective-permute-start(bf16[2,1024,256]{2,1,0:T(8,128)(2,1)S(1)} %maximum_select_fusion.5), channel_id=1, source_target_pairs={{0,64},{32,96},{64,0},{96,32},{128,192},{160,224},{192,128},{224,1... | collective-permute-start | bytes 3145736 | tf_op jit(solution)/shard_map/ppermute | solution.py:10
  367.5 6.5 %copy-start.15 = (bf16[1,64,1024]{2,1,0:T(8,128)(2,1)S(1)}, bf16[1,64,1024]{2,1,0:T(8,128)(2,1)}, u32[]{:S(2)}) copy-start(bf16[1,64,1024]{2,1,0:T(8,128)(2,1)} %param.29) | copy-start | bytes 393220
  377.6 26.4 %copy-start.10 = (bf16[256,64]{0,1:T(8,128)(2,1)}, bf16[256,64]{0,1:T(8,128)(2,1)S(1)}, u32[]{:S(2)}) copy-start(bf16[256,64]{0,1:T(8,128)(2,1)S(1)} %fusion.8) | copy-start | bytes 98308
  378.8 22.1 %all-to-all-start.6 = ((bf16[32,1,64,256]{3,2,1,0:T(8,128)(2,1)}), bf16[32,1,64,256]{3,2,1,0:T(8,128)(2,1)}, u32[]{:S(2)}, u32[]{:S(2)}) async-start(bf16[32,1,64,256]{3,2,1,0:T(8,128)(2,1)} %stack.20), calls=%async_computation.6 | async-start | bytes 2097152 | tf_op jit(solution)/shard_map/all_to_all | solution.py:27
  400.9 3.2 copy-start.5
  400.9 26.6 %collective-permute-start.8 = (bf16[1,2048,256]{2,1,0:T(8,128)(2,1)}, bf16[1,2048,256]{2,1,0:T(8,128)(2,1)S(1)}, u32[]{:S(2)}, u32[]{:S(2)}) collective-permute-start(bf16[1,2048,256]{2,1,0:T(8,128)(2,1)} %bitcast.40), channel_id=1, source_target_pairs={{0,32},{32,0},{64,96},{96,64},{128,160},{160,128},{192,224},{224,1... | collective-permute-start | bytes 3145736 | tf_op jit(solution)/shard_map/ppermute | solution.py:10
  404.1 1.6 copy-start.2
  404.1 1.7 copy-start.6
  405.7 1.6 copy-start.4
  405.7 1.6 copy-start.9
